TPU v7x, 256 devices: a whole 4x4x8 slice. The times are simulated.
256 devices in a mesh: seq: 64 (over x, z, core), grp: 4 (over y).
Axes of the slice: x: 4, y: 4, z: 8, core: 2. Of those that a mesh axis runs over, the one named last changes fastest.
Arguments:
- queries: bfloat16 [4, 8192, 640], P('grp', 'seq'), may hold values from -120 to 120
- comp_kv: bfloat16 [4, 8192, 256], P('grp', 'seq'), may hold values from -6 to 6
- out_grad: bfloat16 [4, 8192, 640], P('grp', 'seq'), may hold values from -6 to 6
- comp_ids: int32 [4, 8192], P('grp', 'seq'), may hold values from 0 to 7, as said below
- comp_pos: int32 [4, 8192], P('grp', 'seq'), may hold values from 0 to 4095, as said below
- prompt_kv: bfloat16 [4, 4096, 256], P('grp', 'seq'), may hold values from -6 to 6
- owned_prompt: int32 [4], replicated, may hold values from 0 to 3, each once
Outputs:
- grad_queries: bfloat16 [4, 8192, 640], P('grp', 'seq')
- grad_comp_kv: bfloat16 [4, 8192, 256], P('grp', 'seq')
- grad_prompt_kv: bfloat16 [4, 4096, 256], P('grp', 'seq')
Inputs may be any that keep to these rules, and one draw needn't show every extreme that they name: `comp_ids`: completions 0 to 7 each hold whole blocks of 32 consecutive positions; each is packed in blocks of 32 tokens in an arbitrary order over the token axis; the longest completion has exactly 128 blocks. `comp_pos`: the tokens of one completion hold positions 0 to its length minus one, each once.
All inputs are finite; a program needn't handle non-finite values.
Results may differ from a plain program's by a relative error of at most 0.005.
Values may be sent and summed in bfloat16 or wider, within the bound.
A program may use at most 128 MiB of HBM per device.

v0:
```python
import math

import jax
import jax.numpy as jnp
from jax import lax
from jax.sharding import PartitionSpec as P

KBLK = 512


def shards(queries, comp_kv, out_grad, comp_ids, comp_pos, prompt_kv, owned_prompt):
    query_rows = queries[0]
    tokens_here = query_rows.shape[0]
    head_size = comp_kv.shape[2] // 2
    heads = query_rows.shape[1] // head_size
    group = lax.axis_index("grp")
    slots = lax.all_gather(prompt_kv, "grp", axis=0, tiled=True)
    pick = owned_prompt == group
    mine = jnp.sum(jnp.where(pick[:, None, None], slots, jnp.zeros_like(slots)), 0)
    whole_prompt, whole_comp, ids_all, pos_all = (
        lax.all_gather(mine, "seq", axis=0, tiled=True),
        lax.all_gather(comp_kv[0], "seq", axis=0, tiled=True),
        lax.all_gather(comp_ids[0], "seq", axis=0, tiled=True),
        lax.all_gather(comp_pos[0], "seq", axis=0, tiled=True),
    )
    plen_all = whole_prompt.shape[0]
    keys_all = jnp.concatenate([whole_prompt, whole_comp], 0)
    key_ids = jnp.concatenate([jnp.full((plen_all,), -1, jnp.int32), ids_all])
    key_pos = jnp.concatenate([jnp.full((plen_all,), -1, jnp.int32), pos_all])
    total_keys = keys_all.shape[0]
    nblocks = total_keys // KBLK
    prompt_blocks = plen_all // KBLK
    query_heads = query_rows.reshape(tokens_here, heads, head_size)
    grad_heads = out_grad[0].reshape(tokens_here, heads, head_size)
    query_ids = comp_ids[0]
    query_pos = comp_pos[0]
    scale = 1.0 / math.sqrt(head_size)

    def block_scores(start, count):
        kslice = lax.dynamic_slice_in_dim(keys_all, start, count, 0)
        kid = lax.dynamic_slice_in_dim(key_ids, start, count, 0)
        kpos = lax.dynamic_slice_in_dim(key_pos, start, count, 0)
        logits = (
            jnp.einsum(
                "thd,kd->thk",
                query_heads,
                kslice[:, :head_size],
                preferred_element_type=jnp.float32,
            )
            * scale
        )
        visible = (kid[None, :] == -1) | (kid[None, :] == query_ids[:, None]) & (
            kpos[None, :] <= query_pos[:, None]
        )
        logits = jnp.where(visible[:, None, :], logits, -1e30)
        dprobs = jnp.einsum(
            "thd,kd->thk", grad_heads, kslice[:, head_size:], preferred_element_type=jnp.float32
        )
        return (logits, dprobs, kslice)

    def stats_step(carry, index):
        highest, total, weighted = carry
        logits, dprobs, unused = block_scores(index * KBLK, KBLK)
        new_high = jnp.maximum(highest, jnp.max(logits, -1))
        shrink = jnp.exp(highest - new_high)
        expo = jnp.exp(logits - new_high[..., None])
        total = total * shrink + jnp.sum(expo, -1)
        weighted = weighted * shrink + jnp.sum(expo * dprobs, -1)
        return ((new_high, total, weighted), None)

    start_stats = (
        jnp.full((tokens_here, heads), -1e30, jnp.float32),
        jnp.zeros((tokens_here, heads), jnp.float32),
        jnp.zeros((tokens_here, heads), jnp.float32),
    )
    block_index = jnp.arange(nblocks, dtype=jnp.int32)
    prompt_index = jnp.arange(prompt_blocks, dtype=jnp.int32)
    comp_index = jnp.arange(prompt_blocks, nblocks, dtype=jnp.int32)
    (highest, total, weighted), unused = lax.scan(stats_step, start_stats, block_index)
    lse = highest + jnp.log(total)
    delta = weighted / total

    def block_grads(start, count):
        logits, dprobs, kslice = block_scores(start, count)
        probs = jnp.exp(logits - lse[..., None])
        dlogits = probs * (dprobs - delta[..., None])
        return (probs.astype(jnp.bfloat16), dlogits.astype(jnp.bfloat16), kslice)

    def key_terms(probs_low, dlog_low):
        grad_k = (
            jnp.einsum("thk,thd->kd", dlog_low, query_heads, preferred_element_type=jnp.float32)
            * scale
        )
        grad_v = jnp.einsum(
            "thk,thd->kd", probs_low, grad_heads, preferred_element_type=jnp.float32
        )
        return jnp.concatenate([grad_k, grad_v], 1)

    def query_term(dlog_low, kslice):
        return jnp.einsum(
            "thk,kd->thd", dlog_low, kslice[:, :head_size], preferred_element_type=jnp.float32
        )

    def full_step(carry, index):
        probs_low, dlog_low, kslice = block_grads(index * KBLK, KBLK)
        return (carry + query_term(dlog_low, kslice), key_terms(probs_low, dlog_low))

    start_query = jnp.zeros((tokens_here, heads, head_size), jnp.float32)
    grad_query, prompt_stack = lax.scan(full_step, start_query, prompt_index)
    grad_query, comp_stack = lax.scan(full_step, grad_query, comp_index)
    comp_local = comp_stack.reshape(total_keys - plen_all, 2 * head_size)
    prompt_local = prompt_stack.reshape(plen_all, 2 * head_size)
    prompt_sum, comp_sum = (
        lax.psum_scatter(prompt_local, "seq", scatter_dimension=0, tiled=True),
        lax.psum_scatter(comp_local, "seq", scatter_dimension=0, tiled=True),
    )
    grad_queries = (
        (grad_query * scale).astype(jnp.bfloat16).reshape(1, tokens_here, heads * head_size)
    )
    grad_comp = comp_sum.astype(jnp.bfloat16)[None]
    own_prompt = prompt_sum.astype(jnp.bfloat16)[None]
    returned = lax.all_gather(own_prompt, "grp", axis=0, tiled=True)
    wanted = owned_prompt[group]
    choose = jnp.arange(returned.shape[0], dtype=jnp.int32) == wanted
    slotted = jnp.sum(jnp.where(choose[:, None, None], returned, jnp.zeros_like(returned)), 0)
    return (grad_queries, grad_comp, slotted[None])


def solution(mesh):
    placed = (
        P("grp", "seq", None),
        P("grp", "seq", None),
        P("grp", "seq", None),
        P("grp", "seq"),
        P("grp", "seq"),
        P("grp", "seq", None),
        P(),
    )
    return jax.shard_map(
        shards,
        mesh=mesh,
        in_specs=placed,
        out_specs=(P("grp", "seq", None), P("grp", "seq", None), P("grp", "seq", None)),
        check_vma=False,
    )
```

profile of v0, /device:TPU:1, one launch (start us, length us, event | category | flops | bytes accessed | tf_op | source)
XLA Modules:
  0.0 656.2 jit_solution(2588047924226946761)
XLA Ops:
  7.2 10.9 %all_gather.20 = bf16[4,64,256]{2,1,0:T(8,128)(2,1)S(1)} all-gather(bf16[1,64,256]{2,1,0:T(8,128)(2,1)} %param.18), channel_id=1, replica_groups=mesh['seq'=64,'grp'=4] {'grp'}, dimensions={0}, use_global_device_ids=true | all-gather | bytes 163840 | tf_op jit(solution)/shard_map/all_gather | solution.py:17
  20.4 45.9 %all-gather = s32[1,8192]{1,0:T(1,128)S(1)} all-gather(s32[1,128]{1,0:T(1,128)} %param.16), channel_id=2, replica_groups=mesh['seq'=64,'grp'=4] {'seq'}, dimensions={1}, use_global_device_ids=true | all-gather | bytes 33280 | tf_op jit(solution)/shard_map/all_gather | solution.py:23
  66.3 37.3 %all-gather.1 = s32[1,8192]{1,0:T(1,128)S(1)} all-gather(s32[1,128]{1,0:T(1,128)} %param.17), channel_id=3, replica_groups=mesh['seq'=64,'grp'=4] {'seq'}, dimensions={1}, use_global_device_ids=true | all-gather | bytes 33280 | tf_op jit(solution)/shard_map/all_gather | solution.py:24
  105.3 76.6 %all-gather.9.cloned.1.call-done = bf16[1,8192,256]{2,1,0:T(8,128)(2,1)} async-done(((bf16[1,128,256]{2,1,0:T(8,128)(2,1)}), bf16[1,8192,256]{2,1,0:T(8,128)(2,1)}) %all-gather.9.cloned.1.call-update) | async-done | bytes 4194320 | tf_op jit(solution)/shard_map/all_gather | solution.py:22
  181.9 8.1 %pad_maximum_fusion = bf16[12288,256]{1,0:T(8,128)(2,1)} fusion(bf16[8192,256]{1,0:T(8,128)(2,1)} %bitcast.201, bf16[4096,256]{1,0:T(8,128)(2,1)} %all-gather.7.cloned.1.call-done), kind=kLoop, calls=%fused_computation.63 | loop fusion | flops 12582912 | bytes 12582912 | tf_op jit(solution)/shard_map/concatenate | solution.py:27
  190.0 108.2 %while.41 = (s32[]{:T(128)}, f32[128,5]{0,1:T(8,128)S(1)}, f32[128,5]{0,1:T(8,128)S(1)}, f32[128,5]{0,1:T(8,128)S(1)}, s32[24]{0:T(128)S(1)}, /*index=5*/s32[122...) while((s32[]{:T(128)}, f32[128,5]{0,1:T(8,128)S(1)}, ...), condition=%wide.region_5.6_spmd.clone, body=%wide.region_1.5_spmd.clone.sunk | while | flops 170660736 | bytes 4713738 | solution.py:79
  298.3 59.2 %while.42 = (s32[]{:T(128)}, f32[128,5,128]{2,0,1:T(8,128)S(1)}, f32[8,512,256]{2,1,0:T(8,128)}, s32[8]{0:T(128)S(1)}, s32[12288]{0:T(1024)S(1)}, /*index=5*/s32...) while((s32[]{:T(128)}, f32[128,5,128]{2,0,1:T(8,128)S(1)}, ...), condition=%wide.region_7.8_spmd.clone, body=%wide.region_6.7_spmd.clone.sunk | while | flops 422347264 | bytes 11423001 | solution.py:109
  303.3 1.3 convolution_add_fusion.5
  310.7 1.3 convolution_add_fusion.5
  318.1 1.3 convolution_add_fusion.5
  325.5 1.3 convolution_add_fusion.5
  332.9 1.3 convolution_add_fusion.5
  340.3 1.3 convolution_add_fusion.5
  347.6 1.3 convolution_add_fusion.5
  351.8 1.3 fusion.95
  355.1 1.3 convolution_add_fusion.5
  357.6 118.2 %while.40 = (s32[]{:T(128)}, f32[128,5,128]{2,0,1:T(8,128)S(1)}, f32[16,512,256]{2,1,0:T(8,128)}, s32[16]{0:T(128)S(1)}, s32[12288]{0:T(1024)S(1)}, /*index=5*/s...) while((s32[]{:T(128)}, f32[128,5,128]{2,0,1:T(8,128)S(1)}, ...), condition=%wide.region_9.10_spmd, body=%wide.region_8.9_spmd.sunk | while | flops 422265344 | bytes 11422991 | solution.py:110
  374.0 1.3 fusion.79
  377.3 1.3 convolution_add_fusion.4
  381.4 1.3 fusion.79
  384.7 1.3 convolution_add_fusion.4
  388.8 1.3 fusion.79
  396.2 1.3 fusion.79
  399.5 1.3 convolution_add_fusion.4
  403.6 1.3 fusion.79
  411.0 1.3 fusion.79
  433.2 1.3 fusion.79
  447.9 1.3 fusion.79
  478.7 14.7 %reduce-scatter.5.cloned.1.call-done = f32[64,256]{1,0:T(8,128)} async-done(((f32[4096,256]{1,0:T(8,128)}), f32[64,256]{1,0:T(8,128)}) %reduce-scatter.5.cloned.1.call-update) | async-done | bytes 65552 | tf_op jit(solution)/shard_map/reduce_scatter | solution.py:114
  494.3 9.4 %all-gather.3 = bf16[256,256]{1,0:T(8,128)(2,1)S(1)} all-gather(bf16[64,256]{1,0:T(8,128)(2,1)S(1)} %convert_element_type.27), channel_id=5, replica_groups=mesh['seq'=64,'grp'=4] {'grp'}, dimensions={0}, use_global_device_ids=true | all-gather | bytes 163840 | tf_op jit(solution)/shard_map/all_gather | solution.py:122
  504.4 143.7 %reduce-scatter.3.cloned.1.call-done = f32[128,256]{1,0:T(8,128)} async-done(((f32[8192,256]{1,0:T(8,128)}), f32[128,256]{1,0:T(8,128)}) %reduce-scatter.3.cloned.1.call-update) | async-done | bytes 131088 | tf_op jit(solution)/shard_map/reduce_scatter | solution.py:115
  648.1 1.5 convert_bitcast_fusion
  (550 shorter events, 232.6 us)
Async XLA Ops:
  7.2 97.7 %copy-start = (bf16[1,128,640]{2,1,0:T(8,128)(2,1)S(1)}, bf16[1,128,640]{2,1,0:T(8,128)(2,1)}, u32[]{:S(2)}) copy-start(bf16[1,128,640]{2,1,0:T(8,128)(2,1)} %param.15) | copy-start | bytes 491524
  7.2 98.1 %all-gather.7.cloned.1.call-start = ((), (), s32[]{:S(2)}) async-start(), calls=%async_computation.2 | async-start | bytes 2129920 | tf_op jit(solution)/shard_map/all_gather | solution.py:21
  19.5 162.4 %all-gather.9.cloned.1.call-start = ((), (), s32[]{:S(2)}) async-start(), calls=%async_computation.5 | async-start | bytes 4259840 | tf_op jit(solution)/shard_map/all_gather | solution.py:22
  20.3 473.2 %reduce-scatter.5.cloned.1.call-start = ((), (), s32[]{:S(2)}) async-start(), calls=%async_computation.4 | async-start | bytes 4259840 | tf_op jit(solution)/shard_map/reduce_scatter | solution.py:114
  181.9 8.2 %copy-start.1 = (s32[1,128]{1,0:T(1,128)S(1)}, s32[1,128]{1,0:T(1,128)}, u32[]{:S(2)}) copy-start(s32[1,128]{1,0:T(1,128)} %param.16) | copy-start | bytes 1540
  181.9 8.2 %copy-start.2 = (s32[1,128]{1,0:T(1,128)S(1)}, s32[1,128]{1,0:T(1,128)}, u32[]{:S(2)}) copy-start(s32[1,128]{1,0:T(1,128)} %param.17) | copy-start | bytes 1540
  357.5 290.6 %reduce-scatter.3.cloned.1.call-start = ((), (), s32[]{:S(2)}) async-start(), calls=%async_computation.3 | async-start | bytes 8519680 | tf_op jit(solution)/shard_map/reduce_scatter | solution.py:115
  475.8 0.7 copy-start.3
Sparse Core Ops, SparseCore 0:
  19.6 82.6 all-gather.6
  105.1 76.7 all-gather.8
  357.6 135.7 reduce-scatter.4
  498.1 149.9 reduce-scatter.2
where the time goes:
time: 663 us; the launch traced here: 656 us
  waiting for transfers between devices  236 us (36%)
  matrix products  172 us (26%)
  blocking collectives  104 us (16%)
  local copies, waits for them, and re-layouts  60.7 us (9%)
  other arithmetic  35.9 us (5%)
  loops' own time  34.7 us (5%)
  between operations  13.9 us (2%)
    reduce_scatter x1, waiting for transfers between devices, shards(): lax.psum_scatter(comp_local, 'seq', scatter_dimension=0, tiled=True)  144 us
    all_gather x1, waiting for transfers between devices, shards(): lax.all_gather(comp_kv[0], 'seq', axis=0, tiled=True)  76.6 us
    dot_general x48, matrix products, block_scores(): jnp.einsum('thd,kd->thk', query_heads, kslice[:, :head_size], preferred_e...  62.5 us
    dot_general x48, matrix products, block_scores(): jnp.einsum('thd,kd->thk', grad_heads, kslice[:, head_size:], preferred_el...  60.5 us
    all_gather x1, blocking collectives, shards(): lax.all_gather(comp_ids[0], 'seq', axis=0, tiled=True)  45.9 us
    all_gather x1, blocking collectives, shards(): lax.all_gather(comp_pos[0], 'seq', axis=0, tiled=True)  37.3 us
    dot_general x24, matrix products, query_term(): jnp.einsum('thk,kd->thd', dlog_low, kslice[:, :head_size], preferred_elem...  32 us
    another operation x1, loops' own time, shards(): lax.scan(stats_step, start_stats, block_index)  17.4 us
  transfers between devices with their start and end apart: 4, of which 3 were waited for; matrix products, arithmetic and copies ran while one was open for 17% of the time, Pallas kernels for 0%

commit v1 on v0

v1 whole, which is shorter than its diff:
```python
import math

import jax
import jax.numpy as jnp
from jax import lax
from jax.experimental import pallas as pl
from jax.experimental.pallas import tpu as pltpu
from jax.sharding import PartitionSpec as P

XN = 4
ZN = 8
CN = 2
GN = 4
H = 5
DH = 128
TOK = 128
PTOK = 64
ROWS = H * TOK
UNIT = 512
SPAN = 4096
SCALE = 1.0 / math.sqrt(DH)
C2 = SCALE * 1.4426950408889634
NEG = -1e30
MESH = pl.DeviceIdType.MESH
N_SEM = 112

COMP_AT = [1, 7, 2, 6, 3, 5, 4, 0]
PROMPT_AT = [0, 1, 7, 2, 6, 3, 5, 4]


def comp_slot(o):
    at = COMP_AT.index(o)
    return at // 2, (at % 2) * CN * TOK


def prompt_slot(o):
    at = PROMPT_AT.index(o)
    return 4 + at // 4, (at % 4) * CN * PTOK


def nt(a, b):
    return lax.dot_general(a, b, (((1,), (1,)), ((), ())), preferred_element_type=jnp.float32)


def nn(a, b):
    return lax.dot_general(a, b, (((1,), (0,)), ((), ())), preferred_element_type=jnp.float32)


def tn(a, b):
    return lax.dot_general(a, b, (((0,), (0,)), ((), ())), preferred_element_type=jnp.float32)


def kernel(
    owned,
    ids,
    pos,
    q_in,
    d_in,
    kv_in,
    p_in,
    dq_out,
    dc_out,
    dp_out,
    code,
    gq,
    gd,
    gqc,
    gkc,
    keys,
    wide,
    qs,
    ds,
    slots,
    mine,
    st,
    sbuf,
    norm,
    acc,
    dqt,
    own_c,
    own_p,
    pair_s,
    pair_r,
    zs,
    zin_c,
    zin_p,
    dqs,
    dqr,
    yslots,
    send,
    recv,
    loc,
):
    f32, bf = jnp.float32, jnp.bfloat16
    s_at = lax.axis_index("seq")
    g = lax.axis_index("grp")
    x, z, c = s_at // (ZN * CN), lax.rem(s_at // CN, ZN), lax.rem(s_at, CN)

    def dev(dx, dz, dc, dg=0):
        xx, zz, gg = lax.rem(x + dx, XN), lax.rem(z + dz, ZN), lax.rem(g + dg, GN)
        cc = 1 - c if dc else c
        return (xx * (ZN * CN) + zz * CN + cc, gg)

    everyone = []
    count = [0]

    def start(src, dst, to):
        cp = pltpu.make_async_remote_copy(
            src_ref=src,
            dst_ref=dst,
            send_sem=send.at[count[0]],
            recv_sem=recv.at[count[0]],
            device_id=to,
            device_id_type=MESH,
        )
        count[0] += 1
        cp.start()
        everyone.append(cp)
        return cp

    def got(*cps):
        for cp in cps:
            cp.wait_recv()

    local_n = [0]

    def local(src, dst):
        cp = pltpu.make_async_copy(src, dst, loc.at[local_n[0]])
        local_n[0] += 1
        cp.start()
        return cp

    def comp_rows(o, other, lo=0, n=TOK):
        u, r = comp_slot(o)
        return keys.at[u, pl.ds(r + other * TOK + lo, n)]

    def prompt_rows(o, other, lo=0, n=PTOK):
        u, r = prompt_slot(o)
        return keys.at[u, pl.ds(r + other * PTOK + lo, n)]

    def code_row(o, other):
        u, r = comp_slot(o)
        return gkc.at[u * 4 + r // TOK + other]

    l_q = local(q_in, gq.at[0])
    l_d = local(d_in, gd.at[0])
    l_kv = local(kv_in, comp_rows(0, 0))
    l_p = local(p_in, slots.at[0])
    code[...] = jnp.broadcast_to(ids[...] * SPAN + pos[...], (8, TOK))
    gqc[0] = code[...]
    u0, r0 = comp_slot(0)
    gkc[u0 * 4 + r0 // TOK] = code[...]

    peer = dev(0, 0, 1)
    barrier = pltpu.get_barrier_semaphore()
    friends = [dev(i, 0, 0) for i in range(1, XN)] + [dev(0, 0, 0, i) for i in range(1, GN)]
    friends += [dev(0, i, 0) for i in range(1, ZN)] + [dev(0, i, 1) for i in range(ZN)]
    for to in friends:
        pl.semaphore_signal(barrier, inc=1, device_id=to, device_id_type=MESH)
    pl.semaphore_wait(barrier, len(friends))

    y_cps = [start(p_in, slots.at[GN - i], dev(0, 0, 0, i)) for i in range(1, GN)]
    k_cps = {}
    r_cps = {0: start(kv_in, comp_rows(0, 1), peer)}
    for i in (1, 7):
        k_cps[8 - i] = start(kv_in, comp_rows(8 - i, 0), dev(0, i, 0))
    xq, xd = {}, {}
    for i in (1, 3):
        xq[XN - i] = start(q_in, gq.at[XN - i], dev(i, 0, 0))
        xd[XN - i] = start(d_in, gd.at[XN - i], dev(i, 0, 0))
    for i in (2, 6):
        k_cps[8 - i] = start(kv_in, comp_rows(8 - i, 0), dev(0, i, 0))
    code_cps = [start(code, code_row(0, 1), peer)]
    for i in range(1, ZN):
        code_cps.append(start(code, code_row(ZN - i, 0), dev(0, i, 0)))
        code_cps.append(start(code, code_row(ZN - i, 1), dev(0, i, 1)))
    for i in range(1, XN):
        code_cps.append(start(code, gqc.at[XN - i], dev(i, 0, 0)))

    for i in range(XN):
        st[i, 0:1, :] = jnp.full((1, ROWS), NEG, f32)
        st[i, 1:2, :] = jnp.zeros((1, ROWS), f32)
        st[i, 2:3, :] = jnp.zeros((1, ROWS), f32)

    def spread(i):
        for h in range(H):
            qs[i, h * TOK : (h + 1) * TOK, :] = gq[i, :, h * DH : (h + 1) * DH]
            ds[i, h * TOK : (h + 1) * TOK, :] = gd[i, :, h * DH : (h + 1) * DH]

    def visible(u, i):
        qc = gqc[i, 0:1, :]
        kc = wide[u]
        base = qc - jnp.bitwise_and(qc, SPAN - 1)
        return jnp.concatenate([(kc <= qc) & (kc >= base)] * H, 1)

    def stat_tile(u, i, masked):
        k = keys[u]
        s = nt(k[:, :DH], qs[i])
        if masked:
            s = jnp.where(visible(u, i), s, NEG)
        dp = nt(k[:, DH:], ds[i])
        m = st[i, 0:1, :]
        m2 = jnp.maximum(m, jnp.max(s, 0, keepdims=True) * C2)
        e = jnp.exp2(s * C2 - m2)
        a = jnp.exp2(m - m2)
        st[i, 0:1, :] = m2
        st[i, 1:2, :] = st[i, 1:2, :] * a + jnp.sum(e, 0, keepdims=True)
        st[i, 2:3, :] = st[i, 2:3, :] * a + jnp.sum(e * dp, 0, keepdims=True)

    def loop(n, body):
        def step(j, _):
            body(j)
            return 0

        lax.fori_loop(0, n, step, 0)

    l_p.wait()
    got(*y_cps)
    total = jnp.zeros((PTOK, 2 * DH), f32)
    for i in range(GN):
        w = (owned[lax.rem(g + i, GN)] == g).astype(f32)
        total = total + slots[i].astype(f32) * w
    mine[...] = total.astype(bf)
    p_cps = {}
    rp_cps = {0: start(mine, prompt_rows(0, 1), peer)}
    for i in (1, 7, 2, 6):
        p_cps[8 - i] = start(mine, prompt_rows(8 - i, 0), dev(0, i, 0))
    u, r = prompt_slot(0)
    keys[u, r : r + PTOK, :] = mine[...]

    def relay(o):
        r_cps[o] = start(comp_rows(o, 0), comp_rows(o, 1), peer)

    def relay_p(o):
        rp_cps[o] = start(prompt_rows(o, 0), prompt_rows(o, 1), peer)

    got(k_cps[1], k_cps[7])
    relay(1)
    relay(7)
    got(*code_cps)

    def widen(j):
        wide[j // 4, pl.ds(pl.multiple_of(lax.rem(j, 4) * TOK, TOK), TOK), :] = jnp.broadcast_to(
            gkc[j, 0:1, :], (TOK, TOK)
        ).T

    loop(4 * 4, widen)
    l_q.wait()
    l_d.wait()
    l_kv.wait()
    spread(0)
    got(k_cps[2], k_cps[6])
    relay(2)
    relay(6)
    half, phalf = TOK // 2, PTOK // 2
    k_cps[5] = start(comp_rows(6, 0), comp_rows(5, 0), dev(0, 1, 0))
    k_cps[3] = start(comp_rows(2, 0), comp_rows(3, 0), dev(0, 7, 0))
    far = [
        start(comp_rows(6, 0, 0, half), comp_rows(4, 0, 0, half), dev(0, 2, 0)),
        start(comp_rows(2, 0, half, half), comp_rows(4, 0, half, half), dev(0, 6, 0)),
    ]
    got(r_cps[1], r_cps[7])
    stat_tile(0, 0, True)
    got(p_cps[1], p_cps[7], p_cps[2], p_cps[6])
    p_cps[5] = start(prompt_rows(6, 0), prompt_rows(5, 0), dev(0, 1, 0))
    p_cps[3] = start(prompt_rows(2, 0), prompt_rows(3, 0), dev(0, 7, 0))
    pfar = [
        start(prompt_rows(6, 0, 0, phalf), prompt_rows(4, 0, 0, phalf), dev(0, 2, 0)),
        start(prompt_rows(2, 0, phalf, phalf), prompt_rows(4, 0, phalf, phalf), dev(0, 6, 0)),
    ]
    for o in (1, 7, 2, 6):
        relay_p(o)
    got(xq[3], xd[3], xq[1], xd[1])
    xq[2] = start(gq.at[3], gq.at[2], dev(1, 0, 0))
    xd[2] = start(gd.at[1], gd.at[2], dev(3, 0, 0))
    spread(1)
    spread(3)
    got(r_cps[2], r_cps[6])
    stat_tile(1, 0, True)
    loop(4, lambda j: stat_tile(j // 2, 1 + 2 * lax.rem(j, 2), True))
    got(k_cps[3], k_cps[5], *far)
    for o in (3, 5, 4):
        relay(o)
    got(p_cps[3], p_cps[5], *pfar)
    for o in (3, 5, 4):
        relay_p(o)
    got(rp_cps[0], rp_cps[1], rp_cps[7], rp_cps[2])
    loop(3, lambda j: stat_tile(4, j + j // 2, False))
    got(r_cps[0], r_cps[3], r_cps[5], r_cps[4])
    loop(6, lambda j: stat_tile(2 + j // 3, lax.rem(j, 3) + lax.rem(j, 3) // 2, True))
    got(rp_cps[6], rp_cps[3], rp_cps[5], rp_cps[4])
    loop(3, lambda j: stat_tile(5, j + j // 2, False))
    st_cps = []

    def share(i):
        for j in range(1, XN):
            st_cps.append(start(st.at[i], sbuf.at[XN - 1 - j, (i - j) % XN], dev(j, 0, 0)))

    for i in (0, 1, 3):
        share(i)
    got(xq[2], xd[2])
    spread(2)
    loop(4, lambda u: stat_tile(u, 2, True))
    loop(2, lambda u: stat_tile(4 + u, 2, False))
    share(2)
    dqt[...] = jnp.zeros_like(dqt)
    acc[...] = jnp.zeros_like(acc)
    got(*st_cps)
    for i in range(XN):
        parts = [st[i]] + [sbuf[j, i] for j in range(XN - 1)]
        m = parts[0][0:1]
        for p in parts[1:]:
            m = jnp.maximum(m, p[0:1])
        l = jnp.zeros_like(m)
        w = jnp.zeros_like(m)
        for p in parts:
            a = jnp.exp2(p[0:1] - m)
            l = l + p[1:2] * a
            w = w + p[2:3] * a
        norm[i, 0:1, :] = m + jnp.log2(l)
        norm[i, 1:2, :] = w / l

    def grad_tile(u, i, masked, a):
        kk = keys[u]
        k = kk[:, :DH]
        qrow, drow = qs[i], ds[i]
        p = jnp.exp2(nt(k, qrow) * C2 - norm[i, 0:1, :])
        if masked:
            p = jnp.where(visible(u, i), p, 0.0)
        dl = (p * (nt(kk[:, DH:], drow) - norm[i, 1:2, :])).astype(bf)
        acc[a, :, :DH] += nn(dl, qrow)
        acc[a, :, DH:] += nn(p.astype(bf), drow)
        dqt[i] += tn(k, dl)

    pair_cps, z_cps = {}, {}

    def emit(u, a, own, n, first):
        for t in range(UNIT // (2 * n)):
            r = t * 2 * n
            own[first + t, :, :DH] = acc[a, r : r + n, :DH] * SCALE
            own[first + t, :, DH:] = acc[a, r : r + n, DH:]
            pair_s[u, t * n : (t + 1) * n, :DH] = (acc[a, r + n : r + 2 * n, :DH] * SCALE).astype(bf)
            pair_s[u, t * n : (t + 1) * n, DH:] = acc[a, r + n : r + 2 * n, DH:].astype(bf)
        pair_cps[u] = start(pair_s.at[u], pair_r.at[u], peer)

    def forward(u, own, n, first, at, zin):
        got(pair_cps[u])
        for t in range(UNIT // (2 * n)):
            o = at[first + t]
            both = own[first + t] + pair_r[u, t * n : (t + 1) * n, :].astype(f32)
            if o == 0:
                own[first + t] = both
            else:
                zs[u, t * n : (t + 1) * n, :] = both.astype(bf)
                z_cps[(u, o)] = start(zs.at[u, pl.ds(t * n, n)], zin.at[ZN - 1 - o], dev(0, o, 0))

    loop(4, lambda i: grad_tile(5, i, False, 0))
    emit(5, 0, own_p, PTOK, 4)
    acc[0] = jnp.zeros_like(acc[0])
    loop(4, lambda i: grad_tile(4, i, False, 0))
    emit(4, 0, own_p, PTOK, 0)
    acc[0] = jnp.zeros_like(acc[0])
    forward(5, own_p, PTOK, 4, PROMPT_AT, zin_p)
    loop(4, lambda i: grad_tile(2, i, True, 0))
    emit(2, 0, own_c, TOK, 4)
    acc[0] = jnp.zeros_like(acc[0])
    forward(4, own_p, PTOK, 0, PROMPT_AT, zin_p)
    loop(4, lambda i: grad_tile(1, i, True, 0))
    emit(1, 0, own_c, TOK, 2)
    acc[0] = jnp.zeros_like(acc[0])
    forward(2, own_c, TOK, 4, COMP_AT, zin_c)

    def put_query(i):
        for h in range(H):
            part = dqt[i, :, h * TOK : (h + 1) * TOK].T * SCALE
            dqs[i, :, h * DH : (h + 1) * DH] = part.astype(bf)

    dq_cps = []
    my_cps = []
    for n, i in enumerate((2, 1, 3, 0)):
        loop(2, lambda j: grad_tile(3 * j, i, True, j))
        put_query(i)
        if i:
            dq_cps.append(start(dqs.at[i], dqr.at[XN - 1 - i], dev(i, 0, 0)))
        if n == 0:
            forward(1, own_c, TOK, 2, COMP_AT, zin_c)
        if n == 2:
            got(*[cp for (u, o), cp in z_cps.items() if u >= 4])
            total = own_p[0]
            for j in range(ZN - 1):
                total = total + zin_p[j].astype(f32)
            yslots[0] = total.astype(bf)
            my_cps = [start(yslots.at[0], yslots.at[GN - j], dev(0, 0, 0, j)) for j in range(1, GN)]
    emit(0, 0, own_c, TOK, 0)
    emit(3, 1, own_c, TOK, 6)
    forward(0, own_c, TOK, 0, COMP_AT, zin_c)
    forward(3, own_c, TOK, 6, COMP_AT, zin_c)
    got(*my_cps)
    total = jnp.zeros((PTOK, 2 * DH), f32)
    wanted = owned[g]
    for i in range(GN):
        w = (wanted == lax.rem(g + i, GN)).astype(f32)
        total = total + yslots[i].astype(f32) * w
    dp_out[...] = total.astype(bf)
    got(*dq_cps)
    total = dqs[0].astype(f32)
    for j in range(XN - 1):
        total = total + dqr[j].astype(f32)
    dq_out[...] = total.astype(bf)
    got(*[cp for (u, o), cp in z_cps.items() if u < 4])
    total = own_c[COMP_AT.index(0)]
    for j in range(ZN - 1):
        total = total + zin_c[j].astype(f32)
    dc_out[...] = total.astype(bf)
    for cp in everyone:
        cp.wait_send()


def shards(queries, comp_kv, out_grad, comp_ids, comp_pos, prompt_kv, owned_prompt):
    bf, f32, i32 = jnp.bfloat16, jnp.float32, jnp.int32
    hbm = pl.BlockSpec(memory_space=pl.ANY)
    vmem = pl.BlockSpec(memory_space=pltpu.VMEM)
    smem = pl.BlockSpec(memory_space=pltpu.SMEM)
    grad_q, grad_c, grad_p = pl.pallas_call(
        kernel,
        out_shape=[
            jax.ShapeDtypeStruct((TOK, ROWS), bf),
            jax.ShapeDtypeStruct((TOK, 2 * DH), bf),
            jax.ShapeDtypeStruct((PTOK, 2 * DH), bf),
        ],
        in_specs=[smem, vmem, vmem] + [hbm] * 4,
        out_specs=[vmem] * 3,
        scratch_shapes=[
            pltpu.VMEM((8, TOK), i32),
            pltpu.VMEM((XN, TOK, ROWS), bf),
            pltpu.VMEM((XN, TOK, ROWS), bf),
            pltpu.VMEM((XN, 8, TOK), i32),
            pltpu.VMEM((16, 8, TOK), i32),
            pltpu.VMEM((6, UNIT, 2 * DH), bf),
            pltpu.VMEM((4, UNIT, TOK), i32),
            pltpu.VMEM((XN, ROWS, DH), bf),
            pltpu.VMEM((XN, ROWS, DH), bf),
            pltpu.VMEM((GN, PTOK, 2 * DH), bf),
            pltpu.VMEM((PTOK, 2 * DH), bf),
            pltpu.VMEM((XN, 8, ROWS), f32),
            pltpu.VMEM((XN - 1, XN, 8, ROWS), f32),
            pltpu.VMEM((XN, 8, ROWS), f32),
            pltpu.VMEM((2, UNIT, 2 * DH), f32),
            pltpu.VMEM((XN, DH, ROWS), f32),
            pltpu.VMEM((ZN, TOK, 2 * DH), f32),
            pltpu.VMEM((ZN, PTOK, 2 * DH), f32),
            pltpu.VMEM((6, UNIT // 2, 2 * DH), bf),
            pltpu.VMEM((6, UNIT // 2, 2 * DH), bf),
            pltpu.VMEM((6, UNIT // 2, 2 * DH), bf),
            pltpu.VMEM((ZN - 1, TOK, 2 * DH), bf),
            pltpu.VMEM((ZN - 1, PTOK, 2 * DH), bf),
            pltpu.VMEM((XN, TOK, ROWS), bf),
            pltpu.VMEM((XN - 1, TOK, ROWS), bf),
            pltpu.VMEM((GN, PTOK, 2 * DH), bf),
            pltpu.SemaphoreType.DMA((N_SEM,)),
            pltpu.SemaphoreType.DMA((N_SEM,)),
            pltpu.SemaphoreType.DMA((4,)),
        ],
        compiler_params=pltpu.CompilerParams(
            collective_id=0, has_side_effects=True, vmem_limit_bytes=60 * 1024 * 1024
        ),
    )(owned_prompt, comp_ids, comp_pos, queries[0], out_grad[0], comp_kv[0], prompt_kv[0])
    return grad_q[None], grad_c[None], grad_p[None]


def solution(mesh):
    placed = (
        P("grp", "seq", None),
        P("grp", "seq", None),
        P("grp", "seq", None),
        P("grp", "seq"),
        P("grp", "seq"),
        P("grp", "seq", None),
        P(),
    )
    return jax.shard_map(
        shards,
        mesh=mesh,
        in_specs=placed,
        out_specs=(P("grp", "seq", None), P("grp", "seq", None), P("grp", "seq", None)),
        check_vma=False,
    )
```

time: 663 us -> 88 us (0.13); the launches traced: 656 us -> 87.8 us
  waiting for transfers between devices: 236 us -> 0 us
  matrix products: 172 us -> 0 us
  blocking collectives: 104 us -> 0 us
  Pallas kernels: 0 us -> 84.2 us
  local copies, waits for them, and re-layouts: 60.7 us -> 3 us
  other arithmetic: 35.9 us -> 0 us
  loops' own time: 34.7 us -> 0 us
  between operations: 13.9 us -> 0.65 us
    dot_general x168 -> x0, matrix products: 172 us -> none  [the longest x48 62.5 us: block_scores(): jnp.einsum('thd,kd->thk', query_heads, kslice[:, :head_size], preferred_e...]
    reduce_scatter x2 -> x0, waiting for transfers between devices: 158 us -> none  [the longest x1 144 us: shards(): lax.psum_scatter(comp_local, 'seq', scatter_dimension=0, tiled=True)]
    all_gather x4 -> x0, blocking collectives: 104 us -> none  [the longest x1 45.9 us: shards(): lax.all_gather(comp_ids[0], 'seq', axis=0, tiled=True)]
    pallas_call x0 -> x1, Pallas kernels: none -> 84.2 us  [shards(): pl.pallas_call(kernel, out_shape=[jax.ShapeDtypeStruct((TOK, ROWS), bf),...]
    all_gather x2 -> x0, waiting for transfers between devices: 76.6 us -> none  [the longest x1 76.6 us: shards(): lax.all_gather(comp_kv[0], 'seq', axis=0, tiled=True)]
    another operation x3 -> x0, loops' own time: 34.7 us -> none  [the longest x1 17.4 us: shards(): lax.scan(stats_step, start_stats, block_index)]
    dynamic_slice x97 -> x0, local copies, waits for them, and re-layouts: 32.5 us -> none  [the longest x24 14.1 us: shards(): lax.scan(stats_step, start_stats, block_index)]
    dynamic_update_slice x48 -> x0, local copies, waits for them, and re-layouts: 24.9 us -> none  [the longest x32 16.6 us: shards(): grad_query, comp_stack = lax.scan(full_step, grad_query, comp_index)]
  transfers between devices with their start and end apart: 4 -> 0, of which waited for: 3 -> 0; matrix products, arithmetic and copies ran while one was open for 17% -> 0% of each run, Pallas kernels for 0% -> 0%
where the time goes in v1:
time: 88 us; the launch traced here: 87.8 us
  Pallas kernels  84.2 us (96%)
  local copies, waits for them, and re-layouts  3 us (3%)
    pallas_call x1, Pallas kernels, shards(): pl.pallas_call(kernel, out_shape=[jax.ShapeDtypeStruct((TOK, ROWS), bf),...  84.2 us
    unnamed x7, local copies, waits for them, and re-layouts  3 us

profile of v1, /device:TPU:1, one launch (start us, length us, event | category | flops | bytes accessed | tf_op | source)
XLA Modules:
  0.0 87.8 jit_solution(10681627065873729828)
XLA Ops:
  0.6 84.2 %shard_map.94 = (bf16[128,640]{1,0:T(8,128)(2,1)}, bf16[128,256]{1,0:T(8,128)(2,1)}, bf16[64,256]{1,0:T(8,128)(2,1)}) custom-call(s32[4]{0:T(128)} %owned.1, s32[1,128]{1,0:T(1,128)} %ids.1, s32[1,128]{1,0:T(1,128)} %pos.1, bf16[128,640]{1,0:T(8,128)(2,1)} %bitcast.7, bf16[128,640]{1,0:T(8,128)(2,1)} %bitcast.8, bf16[128,256]{1,0:T(8,128)(2,1)} %bitcast.11, ...), custom_call_target="tpu_custom_call" | custom-call | tf_op jit(solution)/shard_map/pallas_call | solution.py:424
  84.8 0.0 copy-start
  84.8 1.6 %copy.13 = bf16[1,128,640]{2,1,0:T(8,128)(2,1)} copy(bf16[1,128,640]{2,1,0:T(8,128)(2,1)} %bitcast.9) | data formatting | bytes 327680
  86.4 0.0 copy-done
  86.5 0.0 copy-start.1
  86.5 0.6 copy.14
  87.1 0.1 copy-done.1
  87.2 0.6 copy.15
Async XLA Ops:
  84.8 1.6 %copy-start = (bf16[128,256]{1,0:T(8,128)(2,1)S(1)}, bf16[128,256]{1,0:T(8,128)(2,1)}, u32[]{:S(2)}) copy-start(bf16[128,256]{1,0:T(8,128)(2,1)} %get-tuple-element.7) | copy-start | bytes 196612
  86.5 0.8 copy-start.1

commit v2 on v1

v2 whole, which is shorter than its diff:
```python
import math

import jax
import jax.numpy as jnp
from jax import lax
from jax.experimental import pallas as pl
from jax.experimental.pallas import tpu as pltpu
from jax.sharding import PartitionSpec as P

XN = 4
ZN = 8
CN = 2
GN = 4
H = 5
DH = 128
TOK = 128
PTOK = 64
ROWS = H * TOK
UNIT = 512
SPAN = 4096
SCALE = 1.0 / math.sqrt(DH)
C2 = SCALE * 1.4426950408889634
NEG = -1e30
MESH = pl.DeviceIdType.MESH
N_SEM = 112

COMP_AT = [1, 7, 2, 6, 3, 5, 4, 0]
PROMPT_AT = [0, 1, 7, 2, 6, 3, 5, 4]
PAIRS = [(1, 3), (0, 2)]
WIDE = 2 * ROWS


def token_slot(i):
    for p, pair in enumerate(PAIRS):
        if i in pair:
            return p, pair.index(i) * ROWS


def comp_slot(o):
    at = COMP_AT.index(o)
    return at // 2, (at % 2) * CN * TOK


def prompt_slot(o):
    at = PROMPT_AT.index(o)
    return 4 + at // 4, (at % 4) * CN * PTOK


def nt(a, b):
    return lax.dot_general(a, b, (((1,), (1,)), ((), ())), preferred_element_type=jnp.float32)


def nn(a, b):
    return lax.dot_general(a, b, (((1,), (0,)), ((), ())), preferred_element_type=jnp.float32)


def tn(a, b):
    return lax.dot_general(a, b, (((0,), (0,)), ((), ())), preferred_element_type=jnp.float32)


def kernel(
    owned,
    ids,
    pos,
    q_in,
    d_in,
    kv_in,
    p_in,
    dq_out,
    dc_out,
    dp_out,
    code,
    gq,
    gd,
    gqc,
    gkc,
    keys,
    wide,
    qs,
    ds,
    slots,
    mine,
    st,
    sbuf,
    norm,
    logit,
    acc,
    dqt,
    own_c,
    own_p,
    pair_s,
    pair_r,
    zs,
    zin_c,
    zin_p,
    dqs,
    dqr,
    yslots,
    send,
    recv,
    loc,
):
    f32, bf = jnp.float32, jnp.bfloat16
    s_at = lax.axis_index("seq")
    g = lax.axis_index("grp")
    x, z, c = s_at // (ZN * CN), lax.rem(s_at // CN, ZN), lax.rem(s_at, CN)

    def dev(dx, dz, dc, dg=0):
        xx, zz, gg = lax.rem(x + dx, XN), lax.rem(z + dz, ZN), lax.rem(g + dg, GN)
        cc = 1 - c if dc else c
        return (xx * (ZN * CN) + zz * CN + cc, gg)

    everyone = []
    count = [0]

    def start(src, dst, to):
        cp = pltpu.make_async_remote_copy(
            src_ref=src,
            dst_ref=dst,
            send_sem=send.at[count[0]],
            recv_sem=recv.at[count[0]],
            device_id=to,
            device_id_type=MESH,
        )
        count[0] += 1
        cp.start()
        everyone.append(cp)
        return cp

    def got(*cps):
        for cp in cps:
            cp.wait_recv()

    local_n = [0]

    def local(src, dst):
        cp = pltpu.make_async_copy(src, dst, loc.at[local_n[0]])
        local_n[0] += 1
        cp.start()
        return cp

    def comp_rows(o, other, lo=0, n=TOK):
        u, r = comp_slot(o)
        return keys.at[u, pl.ds(r + other * TOK + lo, n)]

    def prompt_rows(o, other, lo=0, n=PTOK):
        u, r = prompt_slot(o)
        return keys.at[u, pl.ds(r + other * PTOK + lo, n)]

    def code_row(o, other):
        u, r = comp_slot(o)
        return gkc.at[u * 4 + r // TOK + other]

    l_q = local(q_in, gq.at[0])
    l_d = local(d_in, gd.at[0])
    l_kv = local(kv_in, comp_rows(0, 0))
    l_p = local(p_in, slots.at[0])
    code[...] = jnp.broadcast_to(ids[...] * SPAN + pos[...], (8, TOK))
    gqc[0] = code[...]
    u0, r0 = comp_slot(0)
    gkc[u0 * 4 + r0 // TOK] = code[...]

    peer = dev(0, 0, 1)
    barrier = pltpu.get_barrier_semaphore()
    friends = [dev(i, 0, 0) for i in range(1, XN)] + [dev(0, 0, 0, i) for i in range(1, GN)]
    friends += [dev(0, i, 0) for i in range(1, ZN)] + [dev(0, i, 1) for i in range(ZN)]
    for to in friends:
        pl.semaphore_signal(barrier, inc=1, device_id=to, device_id_type=MESH)
    acc[...] = jnp.zeros_like(acc)
    dqt[...] = jnp.zeros_like(dqt)
    for p in range(2):
        st[p, 0:1, :] = jnp.full((1, WIDE), NEG, f32)
        st[p, 1:8, :] = jnp.zeros((7, WIDE), f32)
    for cp in (l_p, l_kv, l_q, l_d):
        cp.wait()
    pl.semaphore_wait(barrier, len(friends))

    y_cps = [start(slots.at[0], slots.at[GN - i], dev(0, 0, 0, i)) for i in range(1, GN)]
    code_cps = [start(code, code_row(0, 1), peer)]
    for i in range(1, ZN):
        code_cps.append(start(code, code_row(ZN - i, 0), dev(0, i, 0)))
        code_cps.append(start(code, code_row(ZN - i, 1), dev(0, i, 1)))
    for i in range(1, XN):
        code_cps.append(start(code, gqc.at[XN - i], dev(i, 0, 0)))
    k_cps, r_cps, p_cps, rp_cps, xq, xd = {}, {}, {}, {}, {}, {}
    mine_k = comp_rows(0, 0)
    xq[3] = start(gq.at[0], gq.at[3], dev(1, 0, 0))
    xd[1] = start(gd.at[0], gd.at[1], dev(3, 0, 0))
    for i in (1, 7):
        k_cps[8 - i] = start(mine_k, comp_rows(8 - i, 0), dev(0, i, 0))
    r_cps[0] = start(mine_k, comp_rows(0, 1), peer)
    for i in (2, 6):
        k_cps[8 - i] = start(mine_k, comp_rows(8 - i, 0), dev(0, i, 0))
    xd[3] = start(gd.at[0], gd.at[3], dev(1, 0, 0))
    xq[1] = start(gq.at[0], gq.at[1], dev(3, 0, 0))

    def relay(*os):
        for o in os:
            r_cps[o] = start(comp_rows(o, 0), comp_rows(o, 1), peer)

    def relay_p(*os):
        for o in os:
            rp_cps[o] = start(prompt_rows(o, 0), prompt_rows(o, 1), peer)

    def loop(n, body):
        def step(j, _):
            body(j)
            return 0

        lax.fori_loop(0, n, step, 0)

    def widen(j):
        wide[j // 4, pl.ds(pl.multiple_of(lax.rem(j, 4) * TOK, TOK), TOK), :] = jnp.broadcast_to(
            gkc[j, 0:1, :], (TOK, TOK)
        ).T

    def spread(i):
        p, at = token_slot(i)
        for h in range(H):
            rows = slice(at + h * TOK, at + (h + 1) * TOK)
            qs[p, rows, :] = gq[i, :, h * DH : (h + 1) * DH]
            ds[p, rows, :] = gd[i, :, h * DH : (h + 1) * DH]

    def visible(u, p):
        masks = []
        for i in PAIRS[p]:
            qc = gqc[i, 0:1, :]
            kc = wide[u]
            base = qc - jnp.bitwise_and(qc, SPAN - 1)
            masks += [(kc <= qc) & (kc >= base)] * H
        return jnp.concatenate(masks, 1)

    def stat_tile(u, p, masked):
        k = keys[u]
        s = nt(k[:, :DH], qs[p])
        if masked:
            s = jnp.where(visible(u, p), s, NEG)
        s = s * C2
        logit[u, p] = s
        dp = nt(k[:, DH:], ds[p])
        m = st[p, 0:1, :]
        m2 = jnp.maximum(m, jnp.max(s, 0, keepdims=True))
        e = jnp.exp2(s - m2)
        a = jnp.exp2(m - m2)
        st[p, 0:1, :] = m2
        st[p, 1:2, :] = st[p, 1:2, :] * a + jnp.sum(e, 0, keepdims=True)
        st[p, 2:3, :] = st[p, 2:3, :] * a + jnp.sum(e * dp, 0, keepdims=True)

    spread(0)
    got(*y_cps)
    total = jnp.zeros((PTOK, 2 * DH), f32)
    for i in range(GN):
        w = (owned[lax.rem(g + i, GN)] == g).astype(f32)
        total = total + slots[i].astype(f32) * w
    mine[...] = total.astype(bf)
    for i in (1, 7, 2, 6):
        p_cps[8 - i] = start(mine, prompt_rows(8 - i, 0), dev(0, i, 0))
    rp_cps[0] = start(mine, prompt_rows(0, 1), peer)
    u, r = prompt_slot(0)
    keys[u, r : r + PTOK, :] = mine[...]
    got(k_cps[1], k_cps[7])
    relay(1, 7)
    got(*code_cps)
    loop(4 * 4, widen)
    half, phalf = TOK // 2, PTOK // 2
    got(k_cps[2], k_cps[6])
    k_cps[5] = start(comp_rows(6, 0), comp_rows(5, 0), dev(0, 1, 0))
    k_cps[3] = start(comp_rows(2, 0), comp_rows(3, 0), dev(0, 7, 0))
    far = [
        start(comp_rows(6, 0, 0, half), comp_rows(4, 0, 0, half), dev(0, 2, 0)),
        start(comp_rows(2, 0, half, half), comp_rows(4, 0, half, half), dev(0, 6, 0)),
    ]
    relay(2, 6)
    got(xq[3])
    xq[2] = start(gq.at[3], gq.at[2], dev(1, 0, 0))
    got(xd[1])
    xd[2] = start(gd.at[1], gd.at[2], dev(3, 0, 0))
    got(p_cps[1], p_cps[7], p_cps[2], p_cps[6])
    p_cps[5] = start(prompt_rows(6, 0), prompt_rows(5, 0), dev(0, 1, 0))
    p_cps[3] = start(prompt_rows(2, 0), prompt_rows(3, 0), dev(0, 7, 0))
    pfar = [
        start(prompt_rows(6, 0, 0, phalf), prompt_rows(4, 0, 0, phalf), dev(0, 2, 0)),
        start(prompt_rows(2, 0, phalf, phalf), prompt_rows(4, 0, phalf, phalf), dev(0, 6, 0)),
    ]
    relay_p(1, 7, 2, 6)
    got(xd[3], xq[1])
    spread(1)
    spread(3)
    got(r_cps[1], r_cps[7], r_cps[2], r_cps[6])
    loop(2, lambda u: stat_tile(u, 0, True))
    got(k_cps[3], k_cps[5], *far)
    relay(3, 5, 4)
    got(rp_cps[0], rp_cps[1], rp_cps[7], rp_cps[2])
    stat_tile(4, 0, False)
    got(p_cps[3], p_cps[5], *pfar)
    relay_p(3, 5, 4)
    got(r_cps[0], r_cps[3], r_cps[5], r_cps[4])
    loop(2, lambda u: stat_tile(2 + u, 0, True))
    got(rp_cps[6], rp_cps[3], rp_cps[5], rp_cps[4])
    stat_tile(5, 0, False)
    st_cps = []

    def share(i):
        p, at = token_slot(i)
        for j in range(1, XN):
            p2, at2 = token_slot((i - j) % XN)
            to = sbuf.at[XN - 1 - j, p2, :, pl.ds(at2, ROWS)]
            st_cps.append(start(st.at[p, :, pl.ds(at, ROWS)], to, dev(j, 0, 0)))

    share(1)
    share(3)
    got(xq[2], xd[2])
    spread(2)
    loop(4, lambda u: stat_tile(u, 1, True))
    loop(2, lambda u: stat_tile(4 + u, 1, False))
    share(0)
    share(2)
    got(*st_cps)
    for i in range(2):
        parts = [st[i]] + [sbuf[j, i] for j in range(XN - 1)]
        m = parts[0][0:1]
        for p in parts[1:]:
            m = jnp.maximum(m, p[0:1])
        l = jnp.zeros_like(m)
        w = jnp.zeros_like(m)
        for p in parts:
            a = jnp.exp2(p[0:1] - m)
            l = l + p[1:2] * a
            w = w + p[2:3] * a
        norm[i, 0:1, :] = m + jnp.log2(l)
        norm[i, 1:2, :] = w / l

    def grad_tile(e, u, i, lo=0, n=UNIT):
        kk = keys[u, lo : lo + n]
        qrow, drow = qs[i], ds[i]
        p = jnp.exp2(logit[u, i, lo : lo + n] - norm[i, 0:1, :])
        dl = (p * (nt(kk[:, DH:], drow) - norm[i, 1:2, :])).astype(bf)
        acc[e, :n, :DH] += nn(dl, qrow)
        acc[e, :n, DH:] += nn(p.astype(bf), drow)
        dqt[i] += tn(kk[:, :DH], dl)

    pair_cps, z_cps = {}, {}

    def emit(e, n, tiles):
        for t in range(tiles):
            r = (t * 2 + 1) * n
            pair_s[e, t * n : (t + 1) * n, :DH] = (acc[e, r : r + n, :DH] * SCALE).astype(bf)
            pair_s[e, t * n : (t + 1) * n, DH:] = acc[e, r : r + n, DH:].astype(bf)
        rows = pl.ds(0, n * tiles)
        pair_cps[e] = start(pair_s.at[e, rows], pair_r.at[e, rows], peer)

    def forward(e, n, offsets, own, zin):
        got(pair_cps[e])
        for t, o in enumerate(offsets):
            rows = slice(t * n, (t + 1) * n)
            both_k = acc[e, t * 2 * n : (t * 2 + 1) * n, :DH] * SCALE + pair_r[e, rows, :DH].astype(f32)
            both_v = acc[e, t * 2 * n : (t * 2 + 1) * n, DH:] + pair_r[e, rows, DH:].astype(f32)
            if o == 0:
                own[:, :DH] = both_k
                own[:, DH:] = both_v
            else:
                zs[e, rows, :DH] = both_k.astype(bf)
                zs[e, rows, DH:] = both_v.astype(bf)
                z_cps[(e, o)] = start(zs.at[e, pl.ds(t * n, n)], zin.at[ZN - 1 - o], dev(0, o, 0))

    dq_cps = []

    def put_query(i):
        p, at = token_slot(i)
        for h in range(H):
            part = dqt[p, :, at + h * TOK : at + (h + 1) * TOK].T * SCALE
            dqs[i, :, h * DH : (h + 1) * DH] = part.astype(bf)
        if i:
            dq_cps.append(start(dqs.at[i], dqr.at[XN - 1 - i], dev(i, 0, 0)))

    loop(2, lambda i: grad_tile(5, 5, i))
    emit(5, PTOK, 4)
    loop(2, lambda i: grad_tile(4, 4, i))
    emit(4, PTOK, 4)
    forward(5, PTOK, PROMPT_AT[4:], own_p, zin_p)
    loop(2, lambda i: grad_tile(3, 3, i, 0, UNIT // 2))
    emit(3, TOK, 1)
    forward(4, PTOK, PROMPT_AT[:4], own_p, zin_p)
    loop(2, lambda i: grad_tile(2, 2, i))
    emit(2, TOK, 2)
    forward(3, TOK, COMP_AT[6:7], own_c, zin_c)
    loop(2, lambda i: grad_tile(1, 1, i))
    emit(1, TOK, 2)
    forward(2, TOK, COMP_AT[4:6], own_c, zin_c)
    grad_tile(0, 0, 1)
    grad_tile(6, 3, 1, UNIT // 2, UNIT // 2)
    put_query(2)
    forward(1, TOK, COMP_AT[2:4], own_c, zin_c)
    put_query(0)
    got(*[cp for (e, o), cp in z_cps.items() if e in (4, 5)])
    total = own_p[...]
    for j in range(ZN - 1):
        total = total + zin_p[j].astype(f32)
    yslots[0] = total.astype(bf)
    my_cps = [start(yslots.at[0], yslots.at[GN - j], dev(0, 0, 0, j)) for j in range(1, GN)]
    grad_tile(0, 0, 0)
    emit(0, TOK, 2)
    grad_tile(6, 3, 0, UNIT // 2, UNIT // 2)
    emit(6, TOK, 1)
    put_query(1)
    put_query(3)
    forward(0, TOK, COMP_AT[0:2], own_c, zin_c)
    forward(6, TOK, COMP_AT[7:], own_c, zin_c)
    got(*my_cps)
    total = jnp.zeros((PTOK, 2 * DH), f32)
    wanted = owned[g]
    for i in range(GN):
        w = (wanted == lax.rem(g + i, GN)).astype(f32)
        total = total + yslots[i].astype(f32) * w
    dp_out[...] = total.astype(bf)
    got(*dq_cps)
    total = dqs[0].astype(f32)
    for j in range(XN - 1):
        total = total + dqr[j].astype(f32)
    dq_out[...] = total.astype(bf)
    got(*[cp for (e, o), cp in z_cps.items() if e not in (4, 5)])
    total = own_c[...]
    for j in range(ZN - 1):
        total = total + zin_c[j].astype(f32)
    dc_out[...] = total.astype(bf)
    for cp in everyone:
        cp.wait_send()


def shards(queries, comp_kv, out_grad, comp_ids, comp_pos, prompt_kv, owned_prompt):
    bf, f32, i32 = jnp.bfloat16, jnp.float32, jnp.int32
    hbm = pl.BlockSpec(memory_space=pl.ANY)
    vmem = pl.BlockSpec(memory_space=pltpu.VMEM)
    smem = pl.BlockSpec(memory_space=pltpu.SMEM)
    grad_q, grad_c, grad_p = pl.pallas_call(
        kernel,
        out_shape=[
            jax.ShapeDtypeStruct((TOK, ROWS), bf),
            jax.ShapeDtypeStruct((TOK, 2 * DH), bf),
            jax.ShapeDtypeStruct((PTOK, 2 * DH), bf),
        ],
        in_specs=[smem, vmem, vmem] + [hbm] * 4,
        out_specs=[vmem] * 3,
        scratch_shapes=[
            pltpu.VMEM((8, TOK), i32),
            pltpu.VMEM((XN, TOK, ROWS), bf),
            pltpu.VMEM((XN, TOK, ROWS), bf),
            pltpu.VMEM((XN, 8, TOK), i32),
            pltpu.VMEM((16, 8, TOK), i32),
            pltpu.VMEM((6, UNIT, 2 * DH), bf),
            pltpu.VMEM((4, UNIT, TOK), i32),
            pltpu.VMEM((2, WIDE, DH), bf),
            pltpu.VMEM((2, WIDE, DH), bf),
            pltpu.VMEM((GN, PTOK, 2 * DH), bf),
            pltpu.VMEM((PTOK, 2 * DH), bf),
            pltpu.VMEM((2, 8, WIDE), f32),
            pltpu.VMEM((XN - 1, 2, 8, WIDE), f32),
            pltpu.VMEM((2, 8, WIDE), f32),
            pltpu.VMEM((6, 2, UNIT, WIDE), f32),
            pltpu.VMEM((7, UNIT, 2 * DH), f32),
            pltpu.VMEM((2, DH, WIDE), f32),
            pltpu.VMEM((TOK, 2 * DH), f32),
            pltpu.VMEM((PTOK, 2 * DH), f32),
            pltpu.VMEM((7, UNIT // 2, 2 * DH), bf),
            pltpu.VMEM((7, UNIT // 2, 2 * DH), bf),
            pltpu.VMEM((7, UNIT // 2, 2 * DH), bf),
            pltpu.VMEM((ZN - 1, TOK, 2 * DH), bf),
            pltpu.VMEM((ZN - 1, PTOK, 2 * DH), bf),
            pltpu.VMEM((XN, TOK, ROWS), bf),
            pltpu.VMEM((XN - 1, TOK, ROWS), bf),
            pltpu.VMEM((GN, PTOK, 2 * DH), bf),
            pltpu.SemaphoreType.DMA((N_SEM,)),
            pltpu.SemaphoreType.DMA((N_SEM,)),
            pltpu.SemaphoreType.DMA((4,)),
        ],
        compiler_params=pltpu.CompilerParams(
            collective_id=0, has_side_effects=True, vmem_limit_bytes=62 * 1024 * 1024
        ),
    )(owned_prompt, comp_ids, comp_pos, queries[0], out_grad[0], comp_kv[0], prompt_kv[0])
    return grad_q[None], grad_c[None], grad_p[None]


def solution(mesh):
    placed = (
        P("grp", "seq", None),
        P("grp", "seq", None),
        P("grp", "seq", None),
        P("grp", "seq"),
        P("grp", "seq"),
        P("grp", "seq", None),
        P(),
    )
    return jax.shard_map(
        shards,
        mesh=mesh,
        in_specs=placed,
        out_specs=(P("grp", "seq", None), P("grp", "seq", None), P("grp", "seq", None)),
        check_vma=False,
    )
```

time: 88 us -> 72.7 us (0.83)
  Pallas kernels: 84.2 us -> 68.9 us
    pallas_call x1, Pallas kernels: 84.2 us -> 68.9 us  [shards(): pl.pallas_call(kernel, out_shape=[jax.ShapeDtypeStruct((TOK, ROWS), bf),...]
where the time goes in v2:
time: 72.7 us; the launch traced here: 72.5 us
  Pallas kernels  68.9 us (95%)
  local copies, waits for them, and re-layouts  3 us (4%)
    pallas_call x1, Pallas kernels, shards(): pl.pallas_call(kernel, out_shape=[jax.ShapeDtypeStruct((TOK, ROWS), bf),...  68.9 us
    unnamed x7, local copies, waits for them, and re-layouts  3 us

profile of v2, /device:TPU:1, one launch (start us, length us, event | category | flops | bytes accessed | tf_op | source)
XLA Modules:
  0.0 72.5 jit_solution(17297368523175283663)
XLA Ops:
  0.6 68.9 %shard_map.94 = (bf16[128,640]{1,0:T(8,128)(2,1)}, bf16[128,256]{1,0:T(8,128)(2,1)}, bf16[64,256]{1,0:T(8,128)(2,1)}) custom-call(s32[4]{0:T(128)} %owned.1, s32[1,128]{1,0:T(1,128)} %ids.1, s32[1,128]{1,0:T(1,128)} %pos.1, bf16[128,640]{1,0:T(8,128)(2,1)} %bitcast.7, bf16[128,640]{1,0:T(8,128)(2,1)} %bitcast.8, bf16[128,256]{1,0:T(8,128)(2,1)} %bitcast.11, ...), custom_call_target="tpu_custom_call" | custom-call | tf_op jit(solution)/shard_map/pallas_call | solution.py:435
  69.5 0.0 copy-start
  69.5 1.6 %copy.13 = bf16[1,128,640]{2,1,0:T(8,128)(2,1)} copy(bf16[1,128,640]{2,1,0:T(8,128)(2,1)} %bitcast.9) | data formatting | bytes 327680
  71.1 0.0 copy-done
  71.1 0.0 copy-start.1
  71.1 0.6 copy.14
  71.8 0.1 copy-done.1
  71.9 0.6 copy.15
Async XLA Ops:
  69.5 1.6 %copy-start = (bf16[128,256]{1,0:T(8,128)(2,1)S(1)}, bf16[128,256]{1,0:T(8,128)(2,1)}, u32[]{:S(2)}) copy-start(bf16[128,256]{1,0:T(8,128)(2,1)} %get-tuple-element.7) | copy-start | bytes 196612
  71.1 0.8 %copy-start.1 = (bf16[64,256]{1,0:T(8,128)(2,1)S(1)}, bf16[64,256]{1,0:T(8,128)(2,1)}, u32[]{:S(2)}) copy-start(bf16[64,256]{1,0:T(8,128)(2,1)} %get-tuple-element.8) | copy-start | bytes 98308

commit v3 on v2

--- a/solution.py
+++ b/solution.py
@@ -221,30 +221,31 @@
             qs[p, rows, :] = gq[i, :, h * DH : (h + 1) * DH]
             ds[p, rows, :] = gd[i, :, h * DH : (h + 1) * DH]
 
-    def visible(u, p):
+    def visible(u, p, half):
         masks = []
-        for i in PAIRS[p]:
+        for i in PAIRS[p] if half is None else [PAIRS[p][half]]:
             qc = gqc[i, 0:1, :]
             kc = wide[u]
             base = qc - jnp.bitwise_and(qc, SPAN - 1)
             masks += [(kc <= qc) & (kc >= base)] * H
         return jnp.concatenate(masks, 1)
 
-    def stat_tile(u, p, masked):
+    def stat_tile(u, p, masked, half=None):
+        at = slice(0, WIDE) if half is None else slice(half * ROWS, (half + 1) * ROWS)
         k = keys[u]
-        s = nt(k[:, :DH], qs[p])
+        s = nt(k[:, :DH], qs[p, at])
         if masked:
-            s = jnp.where(visible(u, p), s, NEG)
+            s = jnp.where(visible(u, p, half), s, NEG)
         s = s * C2
-        logit[u, p] = s
-        dp = nt(k[:, DH:], ds[p])
-        m = st[p, 0:1, :]
+        logit[u, p, :, at] = s
+        dp = nt(k[:, DH:], ds[p, at])
+        m = st[p, 0:1, at]
         m2 = jnp.maximum(m, jnp.max(s, 0, keepdims=True))
         e = jnp.exp2(s - m2)
         a = jnp.exp2(m - m2)
-        st[p, 0:1, :] = m2
-        st[p, 1:2, :] = st[p, 1:2, :] * a + jnp.sum(e, 0, keepdims=True)
-        st[p, 2:3, :] = st[p, 2:3, :] * a + jnp.sum(e * dp, 0, keepdims=True)
+        st[p, 0:1, at] = m2
+        st[p, 1:2, at] = st[p, 1:2, at] * a + jnp.sum(e, 0, keepdims=True)
+        st[p, 2:3, at] = st[p, 2:3, at] * a + jnp.sum(e * dp, 0, keepdims=True)
 
     spread(0)
     got(*y_cps)
@@ -275,6 +276,14 @@
     xq[2] = start(gq.at[3], gq.at[2], dev(1, 0, 0))
     got(xd[1])
     xd[2] = start(gd.at[1], gd.at[2], dev(3, 0, 0))
+    got(r_cps[1], r_cps[7])
+    stat_tile(0, 1, True, 0)
+    got(r_cps[2], r_cps[6])
+    stat_tile(1, 1, True, 0)
+    got(xd[3], xq[1])
+    spread(1)
+    spread(3)
+    stat_tile(0, 0, True)
     got(p_cps[1], p_cps[7], p_cps[2], p_cps[6])
     p_cps[5] = start(prompt_rows(6, 0), prompt_rows(5, 0), dev(0, 1, 0))
     p_cps[3] = start(prompt_rows(2, 0), prompt_rows(3, 0), dev(0, 7, 0))
@@ -283,21 +292,19 @@
         start(prompt_rows(2, 0, phalf, phalf), prompt_rows(4, 0, phalf, phalf), dev(0, 6, 0)),
     ]
     relay_p(1, 7, 2, 6)
-    got(xd[3], xq[1])
-    spread(1)
-    spread(3)
-    got(r_cps[1], r_cps[7], r_cps[2], r_cps[6])
-    loop(2, lambda u: stat_tile(u, 0, True))
     got(k_cps[3], k_cps[5], *far)
     relay(3, 5, 4)
-    got(rp_cps[0], rp_cps[1], rp_cps[7], rp_cps[2])
-    stat_tile(4, 0, False)
+    stat_tile(1, 0, True)
+    got(r_cps[0], r_cps[3], r_cps[5], r_cps[4])
+    loop(2, lambda u: stat_tile(2 + u, 0, True))
+    got(xq[2], xd[2])
+    spread(2)
     got(p_cps[3], p_cps[5], *pfar)
     relay_p(3, 5, 4)
-    got(r_cps[0], r_cps[3], r_cps[5], r_cps[4])
-    loop(2, lambda u: stat_tile(2 + u, 0, True))
+    loop(2, lambda u: stat_tile(2 + u, 1, True))
+    got(rp_cps[0], rp_cps[1], rp_cps[7], rp_cps[2])
     got(rp_cps[6], rp_cps[3], rp_cps[5], rp_cps[4])
-    stat_tile(5, 0, False)
+    loop(2, lambda u: stat_tile(4 + u, 0, False))
     st_cps = []
 
     def share(i):
@@ -309,9 +316,7 @@
 
     share(1)
     share(3)
-    got(xq[2], xd[2])
-    spread(2)
-    loop(4, lambda u: stat_tile(u, 1, True))
+    loop(2, lambda u: stat_tile(u, 1, True, 1))
     loop(2, lambda u: stat_tile(4 + u, 1, False))
     share(0)
     share(2)
@@ -412,17 +417,17 @@
     for i in range(GN):
         w = (wanted == lax.rem(g + i, GN)).astype(f32)
         total = total + yslots[i].astype(f32) * w
-    dp_out[...] = total.astype(bf)
+    dp_out[...] = total
     got(*dq_cps)
     total = dqs[0].astype(f32)
     for j in range(XN - 1):
         total = total + dqr[j].astype(f32)
-    dq_out[...] = total.astype(bf)
+    dq_out[...] = total
     got(*[cp for (e, o), cp in z_cps.items() if e not in (4, 5)])
     total = own_c[...]
     for j in range(ZN - 1):
         total = total + zin_c[j].astype(f32)
-    dc_out[...] = total.astype(bf)
+    dc_out[...] = total
     for cp in everyone:
         cp.wait_send()
 
@@ -435,9 +440,9 @@
     grad_q, grad_c, grad_p = pl.pallas_call(
         kernel,
         out_shape=[
-            jax.ShapeDtypeStruct((TOK, ROWS), bf),
-            jax.ShapeDtypeStruct((TOK, 2 * DH), bf),
-            jax.ShapeDtypeStruct((PTOK, 2 * DH), bf),
+            jax.ShapeDtypeStruct((TOK, ROWS), f32),
+            jax.ShapeDtypeStruct((TOK, 2 * DH), f32),
+            jax.ShapeDtypeStruct((PTOK, 2 * DH), f32),
         ],
         in_specs=[smem, vmem, vmem] + [hbm] * 4,
         out_specs=[vmem] * 3,
@@ -477,7 +482,7 @@
             collective_id=0, has_side_effects=True, vmem_limit_bytes=62 * 1024 * 1024
         ),
     )(owned_prompt, comp_ids, comp_pos, queries[0], out_grad[0], comp_kv[0], prompt_kv[0])
-    return grad_q[None], grad_c[None], grad_p[None]
+    return grad_q[None].astype(bf), grad_c[None].astype(bf), grad_p[None].astype(bf)
 
 
 def solution(mesh):

time: 72.7 us -> 71.8 us (0.988)
  local copies, waits for them, and re-layouts: 3 us -> 0.01 us
  other arithmetic: 0 us -> 2.95 us
  Pallas kernels: 68.9 us -> 68.1 us
    unnamed x7 -> x4, local copies, waits for them, and re-layouts: 3 us -> 0.01 us
    convert_element_type x0 -> x3, other arithmetic: none -> 2.95 us  [the longest x1 1.7 us: shards(): grad_q[None].astype(bf)]
    pallas_call x1, Pallas kernels: 68.9 us -> 68.1 us  [shards(): pl.pallas_call(kernel, out_shape=[jax.ShapeDtypeStruct((TOK, ROWS), f32),...]
where the time goes in v3:
time: 71.8 us; the launch traced here: 71.7 us
  Pallas kernels  68.1 us (95%)
  other arithmetic  2.95 us (4%)
    pallas_call x1, Pallas kernels, shards(): pl.pallas_call(kernel, out_shape=[jax.ShapeDtypeStruct((TOK, ROWS), f32),...  68.1 us
    convert_element_type x1, other arithmetic, shards(): grad_q[None].astype(bf)  1.7 us

profile of v3, /device:TPU:1, one launch (start us, length us, event | category | flops | bytes accessed | tf_op | source)
XLA Modules:
  0.0 71.7 jit_solution(1486891699159386570)
XLA Ops:
  0.6 68.1 %shard_map.94 = (f32[128,640]{1,0:T(8,128)}, f32[128,256]{1,0:T(8,128)}, f32[64,256]{1,0:T(8,128)}) custom-call(s32[4]{0:T(128)} %owned.1, s32[1,128]{1,0:T(1,128)} %ids.1, s32[1,128]{1,0:T(1,128)} %pos.1, bf16[128,640]{1,0:T(8,128)(2,1)} %bitcast.10, bf16[128,640]{1,0:T(8,128)(2,1)} %bitcast.11, bf16[128,256]{1,0:T(8,128)(2,1)} %bitcast.12, ...), custom_call_target="tpu_custom_call" | custom-call | tf_op jit(solution)/shard_map/pallas_call | solution.py:440
  68.7 0.0 copy-start.1
  68.7 0.0 copy-start
  68.7 1.7 %convert_bitcast_fusion = bf16[1,128,640]{2,1,0:T(8,128)(2,1)} fusion(f32[128,640]{1,0:T(8,128)} %get-tuple-element.6), kind=kLoop, calls=%fused_computation | loop fusion | flops 81920 | bytes 491520 | tf_op jit(solution)/shard_map/convert_element_type | solution.py:485
  70.4 0.0 copy-done.1
  70.4 0.6 convert_bitcast_fusion.2
  71.1 0.0 copy-done
  71.1 0.6 convert_bitcast_fusion.1
Async XLA Ops:
  68.7 1.7 %copy-start.1 = (f32[64,256]{1,0:T(8,128)S(1)}, f32[64,256]{1,0:T(8,128)}, u32[]{:S(2)}) copy-start(f32[64,256]{1,0:T(8,128)} %get-tuple-element.8) | copy-start | bytes 196612
  68.7 2.3 %copy-start = (f32[128,256]{1,0:T(8,128)S(1)}, f32[128,256]{1,0:T(8,128)}, u32[]{:S(2)}) copy-start(f32[128,256]{1,0:T(8,128)} %get-tuple-element.7) | copy-start | bytes 393220
